TPU v7x, 32 devices: a whole 2x2x4 slice. The times are simulated.
32 devices in a mesh: dp: 16 (over z, y, core), tensor: 2 (over x).
Axes of the slice: x: 2, y: 2, z: 4, core: 2. Of those that a mesh axis runs over, the one named last changes fastest.
Arguments:
- tokens: bfloat16 [8192, 1024], P(('dp', 'tensor')), may hold values from -6 to 6
- cotangent: bfloat16 [8192, 1024], P(('dp', 'tensor')), may hold values from -6 to 6
- segment_ids: int32 [8192], P('dp'), may hold values from 0 to 63, never falling along the last dimension, each value on 1 to 512 neighbouring positions
- w_query: bfloat16 [2, 1024, 1024], P(None, 'dp', 'tensor'), may hold values from -0.1875 to 0.1875
- w_key: bfloat16 [2, 1024, 1024], P(None, 'dp', 'tensor'), may hold values from -0.1875 to 0.1875
- w_value: bfloat16 [2, 1024, 1024], P(None, 'dp', 'tensor'), may hold values from -0.1875 to 0.1875
- w_out: bfloat16 [2, 1024, 1024], P(None, ('tensor', 'dp')), may hold values from -0.75 to 0.75
- w_up: bfloat16 [2, 1024, 4096], P(None, 'dp', 'tensor'), may hold values from -0.1875 to 0.1875
- w_down: bfloat16 [2, 4096, 1024], P(None, ('tensor', 'dp')), may hold values from -0.09375 to 0.09375
- qv_bias: bfloat16 [2, 2, 1024], P(None, None, ('tensor', 'dp')), may hold values from -3 to 3
- up_bias: bfloat16 [2, 4096], P(None, ('tensor', 'dp')), may hold values from -3 to 3
- norm_gain: float32 [2, 2, 1024], P(None, None, ('dp', 'tensor')), may hold values from 0.5 to 1.5
- shift_bias: float32 [2, 4, 1024], P(None, None, ('dp', 'tensor')), may hold values from -2 to 2
Outputs:
- output: float32 [8192, 1024], P(('dp', 'tensor'))
- input_grad: float32 [8192, 1024], P(('dp', 'tensor'))
- grad_query: float32 [2, 1024, 1024], P(None, 'dp', 'tensor')
- grad_key: float32 [2, 1024, 1024], P(None, 'dp', 'tensor')
- grad_value: float32 [2, 1024, 1024], P(None, 'dp', 'tensor')
- grad_out: float32 [2, 1024, 1024], P(None, ('tensor', 'dp'))
- grad_up: float32 [2, 1024, 4096], P(None, 'dp', 'tensor')
- grad_down: float32 [2, 4096, 1024], P(None, ('tensor', 'dp'))
- grad_qv_bias: float32 [2, 2, 1024], P(None, None, ('tensor', 'dp'))
- grad_up_bias: float32 [2, 4096], P(None, ('tensor', 'dp'))
- grad_gain: float32 [2, 2, 1024], P(None, None, ('dp', 'tensor'))
- grad_shift: float32 [2, 4, 1024], P(None, None, ('dp', 'tensor'))
Inputs may be any that keep to these rules, and one draw needn't show every extreme that they name: segment_ids never fall along the tokens; every number from 0 up is some token's document, and one document has exactly 512 tokens.
All inputs are finite; a program needn't handle non-finite values.
Results may differ from a plain program's by a relative error of at most 0.034.
Values may be sent and summed in bfloat16 or wider, within the bound.
A program may use at most 192 MiB of HBM per device.

v0:
```python
import jax
import jax.numpy as jnp
from jax import lax
from jax.sharding import PartitionSpec as P

HEAD = 64
LEN = 512


EPS = 1e-06
NEG = -1e30


def layer_norm(z, gain, shift):
    mean = jnp.mean(z, axis=-1, keepdims=True)
    cent = z - mean
    var = jnp.mean(cent * cent, axis=-1, keepdims=True)
    return cent * lax.rsqrt(var + EPS) * gain + shift


def gelu_exact(pre):
    return jax.nn.gelu(pre, approximate=False)


def inner(left, right):
    return lax.dot_general(
        left, right, (((0,), (0,)), ((), ())), preferred_element_type=jnp.float32
    )


def times_back(left, right):
    return lax.dot_general(
        left, right, (((1,), (1,)), ((), ())), preferred_element_type=jnp.float32
    )


def gather_rows(rows):
    return lax.all_gather(rows, "tensor", axis=0, tiled=True)


def gather_grads(rows):
    return lax.all_gather(rows, "tensor", axis=0, tiled=True)


def sum_rows(term, rows):
    return lax.psum_scatter(
        term(jnp.int32(0), lax.axis_size("tensor") * rows).astype(jnp.bfloat16),
        "tensor",
        scatter_dimension=0,
        tiled=True,
    ).astype(jnp.float32)


def sum_grads(term, rows):
    return lax.psum_scatter(
        term(jnp.int32(0), lax.axis_size("tensor") * rows).astype(jnp.bfloat16),
        "tensor",
        scatter_dimension=0,
        tiled=True,
    ).astype(jnp.float32)


def allowed(segment):
    return segment[:, None] == segment[None, :]


def attend_one(args):
    query, key, value, segment = args
    scale = HEAD ** (-0.5)
    scores = jnp.einsum("qhd,khd->hqk", query, key, preferred_element_type=jnp.float32) * scale
    scores = jnp.where(allowed(segment)[None], scores, NEG)
    top = jnp.max(scores, axis=-1, keepdims=True)
    total = top + jnp.log(jnp.sum(jnp.exp(scores - top), axis=-1, keepdims=True))
    probs = jnp.exp(scores - total).astype(jnp.bfloat16)
    result = jnp.einsum("hqk,khd->qhd", probs, value, preferred_element_type=jnp.float32)
    return (result.astype(jnp.bfloat16), total[..., 0])


def attend_back(args):
    query, key, value, segment, total, d_att = args
    scale = HEAD ** (-0.5)
    scores = jnp.einsum("qhd,khd->hqk", query, key, preferred_element_type=jnp.float32) * scale
    scores = jnp.where(allowed(segment)[None], scores, NEG)
    probs = jnp.exp(scores - total[..., None])
    d_probs = jnp.einsum("qhd,khd->hqk", d_att, value, preferred_element_type=jnp.float32)
    row_dot = jnp.sum(d_probs * probs, axis=-1, keepdims=True)
    d_scores = (probs * (d_probs - row_dot)).astype(jnp.bfloat16)
    d_query = (
        jnp.einsum("hqk,khd->qhd", d_scores, key, preferred_element_type=jnp.float32) * scale
    ).astype(jnp.bfloat16)
    d_key = (
        jnp.einsum("hqk,qhd->khd", d_scores, query, preferred_element_type=jnp.float32) * scale
    ).astype(jnp.bfloat16)
    d_value = jnp.einsum(
        "hqk,qhd->khd", probs.astype(jnp.bfloat16), d_att, preferred_element_type=jnp.float32
    ).astype(jnp.bfloat16)
    return (d_query, d_key, d_value)


def forward_layer(stream, mats, vecs, segs, seq):
    w_q, w_k, w_v, w_o, w_u, w_d, qvb, upb = mats
    gains, shifts = vecs
    seqs = segs.shape[0]
    rows = stream.shape[0]
    x_rows = gather_rows(stream.astype(jnp.bfloat16))
    query = (
        jnp.dot(x_rows, w_q, preferred_element_type=jnp.float32) + qvb[0].astype(jnp.float32)
    ).astype(jnp.bfloat16)
    key = jnp.dot(x_rows, w_k, preferred_element_type=jnp.float32).astype(jnp.bfloat16)
    value = (
        jnp.dot(x_rows, w_v, preferred_element_type=jnp.float32) + qvb[1].astype(jnp.float32)
    ).astype(jnp.bfloat16)
    width = query.shape[1]
    local_heads = width // HEAD

    def split(matrix):
        return matrix.reshape(seqs, seq, local_heads, HEAD)

    attended, totals = lax.map(attend_one, (split(query), split(key), split(value), segs))
    attended = attended.reshape(seqs * seq, width)

    def out_term(start, count):
        return jnp.dot(attended, w_o, preferred_element_type=jnp.float32)

    out_sum = sum_rows(out_term, rows)
    mixed = stream + out_sum + shifts[0]
    normed = layer_norm(mixed, gains[0], shifts[1])
    n_rows = gather_rows(normed.astype(jnp.bfloat16))
    pre = jnp.dot(n_rows, w_u, preferred_element_type=jnp.float32) + upb.astype(jnp.float32)
    hidden = gelu_exact(pre).astype(jnp.bfloat16)

    def down_term(start, count):
        return jnp.dot(hidden, w_d, preferred_element_type=jnp.float32)

    down_sum = sum_rows(down_term, rows)
    second = normed + down_sum + shifts[2]
    result = layer_norm(second, gains[1], shifts[3])
    kept = (x_rows, query, key, value, attended, totals, mixed, n_rows, pre, hidden, second)
    return (result, kept)


def backward_layer(grad, mats, vecs, kept, segs, seq):
    w_q, w_k, w_v, w_o, w_u, w_d, qvb, upb = mats
    gains, shifts = vecs
    x_rows, query, key, value, attended, totals, mixed, n_rows, pre, hidden, second = kept
    seqs = segs.shape[0]
    rows = grad.shape[0]
    width = query.shape[1]
    local_heads = width // HEAD

    def split(matrix):
        return matrix.reshape(seqs, seq, local_heads, HEAD)

    _, pull_second = jax.vjp(layer_norm, second, gains[1], shifts[3])
    d_second, d_gain_two, d_shift_two = pull_second(grad)
    d_down_bias = jnp.sum(d_second, axis=0)
    d_f = gather_grads(d_second.astype(jnp.bfloat16))
    grad_down = inner(hidden, d_f)
    d_hidden = times_back(d_f, w_d)
    _, pull_gelu = jax.vjp(gelu_exact, pre)
    d_pre = pull_gelu(d_hidden)[0].astype(jnp.bfloat16)
    grad_up = inner(n_rows, d_pre)
    d_up_bias = jnp.sum(d_pre.astype(jnp.float32), axis=0)

    def up_term(start, count):
        return times_back(d_pre, w_u)

    d_normed = d_second + sum_grads(up_term, rows)
    _, pull_first = jax.vjp(layer_norm, mixed, gains[0], shifts[1])
    d_mixed, d_gain_one, d_shift_one = pull_first(d_normed)
    d_out_bias = jnp.sum(d_mixed, axis=0)
    d_a = gather_grads(d_mixed.astype(jnp.bfloat16))
    grad_out = inner(attended, d_a)
    d_att = times_back(d_a, w_o).astype(jnp.bfloat16)
    d_query, d_key, d_value = lax.map(
        attend_back, (split(query), split(key), split(value), segs, totals, split(d_att))
    )
    d_query = d_query.reshape(seqs * seq, width)
    d_key = d_key.reshape(seqs * seq, width)
    d_value = d_value.reshape(seqs * seq, width)
    grad_q = inner(x_rows, d_query)
    grad_k = inner(x_rows, d_key)
    grad_v = inner(x_rows, d_value)
    d_qv = jnp.stack(
        [jnp.sum(d_query.astype(jnp.float32), axis=0), jnp.sum(d_value.astype(jnp.float32), axis=0)]
    )

    def in_term(start, count):
        part = times_back(d_query, w_q)
        part = part + times_back(d_key, w_k)
        return part + times_back(d_value, w_v)

    d_stream = d_mixed + sum_grads(in_term, rows)
    mat_grads = (grad_q, grad_k, grad_v, grad_out, grad_up, grad_down, d_qv, d_up_bias)
    vec_grads = (
        jnp.stack([d_gain_one, d_gain_two]),
        jnp.stack([d_out_bias, d_shift_one, d_down_bias, d_shift_two]),
    )
    return (d_stream, mat_grads, vec_grads)


def on_device(
    tokens,
    cotangent,
    segment_ids,
    w_query,
    w_key,
    w_value,
    w_out,
    w_up,
    w_down,
    qv_bias,
    up_bias,
    norm_gain,
    shift_bias,
):
    layers = w_query.shape[0]
    group = segment_ids.shape[0]
    seq = min(LEN, group)
    segs = segment_ids.reshape(group // seq, seq)
    stream = tokens.astype(jnp.float32)
    kept_all = []
    mats_all = []
    vecs_all = []
    for layer in range(layers):
        mats = (
            lax.all_gather(w_query[layer], "dp", axis=0, tiled=True),
            lax.all_gather(w_key[layer], "dp", axis=0, tiled=True),
            lax.all_gather(w_value[layer], "dp", axis=0, tiled=True),
            lax.all_gather(w_out[layer], "dp", axis=0, tiled=True),
            lax.all_gather(w_up[layer], "dp", axis=0, tiled=True),
            lax.all_gather(w_down[layer], "dp", axis=0, tiled=True),
            lax.all_gather(qv_bias[layer], "dp", axis=1, tiled=True),
            lax.all_gather(up_bias[layer], "dp", axis=0, tiled=True),
        )
        vecs = (
            lax.all_gather(norm_gain[layer], ("dp", "tensor"), axis=1, tiled=True),
            lax.all_gather(shift_bias[layer], ("dp", "tensor"), axis=1, tiled=True),
        )
        stream, kept = forward_layer(stream, mats, vecs, segs, seq)
        kept_all.append(kept)
        mats_all.append(mats)
        vecs_all.append(vecs)
    grad = cotangent.astype(jnp.float32)
    mat_shards = [None] * layers
    vec_shards = [None] * layers
    for layer in reversed(range(layers)):
        mats = (
            lax.all_gather(w_query[layer], "dp", axis=0, tiled=True),
            lax.all_gather(w_key[layer], "dp", axis=0, tiled=True),
            lax.all_gather(w_value[layer], "dp", axis=0, tiled=True),
            lax.all_gather(w_out[layer], "dp", axis=0, tiled=True),
            lax.all_gather(w_up[layer], "dp", axis=0, tiled=True),
            lax.all_gather(w_down[layer], "dp", axis=0, tiled=True),
            lax.all_gather(qv_bias[layer], "dp", axis=1, tiled=True),
            lax.all_gather(up_bias[layer], "dp", axis=0, tiled=True),
        )
        grad, mat_grads, vec_grads = backward_layer(
            grad, mats, vecs_all[layer], kept_all[layer], segs, seq
        )
        g_q, g_k, g_v, g_o, g_u, g_d, g_qv, g_ub = mat_grads
        mat_shards[layer] = (
            lax.psum_scatter(
                g_q.astype(jnp.bfloat16), "dp", scatter_dimension=0, tiled=True
            ).astype(jnp.float32),
            lax.psum_scatter(
                g_k.astype(jnp.bfloat16), "dp", scatter_dimension=0, tiled=True
            ).astype(jnp.float32),
            lax.psum_scatter(
                g_v.astype(jnp.bfloat16), "dp", scatter_dimension=0, tiled=True
            ).astype(jnp.float32),
            lax.psum_scatter(
                g_o.astype(jnp.bfloat16), "dp", scatter_dimension=0, tiled=True
            ).astype(jnp.float32),
            lax.psum_scatter(
                g_u.astype(jnp.bfloat16), "dp", scatter_dimension=0, tiled=True
            ).astype(jnp.float32),
            lax.psum_scatter(
                g_d.astype(jnp.bfloat16), "dp", scatter_dimension=0, tiled=True
            ).astype(jnp.float32),
            lax.psum_scatter(
                g_qv.astype(jnp.bfloat16), "dp", scatter_dimension=1, tiled=True
            ).astype(jnp.float32),
            lax.psum_scatter(
                g_ub.astype(jnp.bfloat16), "dp", scatter_dimension=0, tiled=True
            ).astype(jnp.float32),
        )
        g_gain, g_shift = vec_grads
        vec_shards[layer] = (
            lax.psum_scatter(g_gain, ("dp", "tensor"), scatter_dimension=1, tiled=True),
            lax.psum_scatter(g_shift, ("dp", "tensor"), scatter_dimension=1, tiled=True),
        )

    def stacked(index, source):
        return jnp.stack([entry[index] for entry in source])

    return (
        stream,
        grad,
        stacked(0, mat_shards),
        stacked(1, mat_shards),
        stacked(2, mat_shards),
        stacked(3, mat_shards),
        stacked(4, mat_shards),
        stacked(5, mat_shards),
        stacked(6, mat_shards),
        stacked(7, mat_shards),
        stacked(0, vec_shards),
        stacked(1, vec_shards),
    )


def solution(mesh):
    in_specs = (
        P(("dp", "tensor"), None),
        P(("dp", "tensor"), None),
        P("dp"),
        P(None, "dp", "tensor"),
        P(None, "dp", "tensor"),
        P(None, "dp", "tensor"),
        P(None, ("tensor", "dp"), None),
        P(None, "dp", "tensor"),
        P(None, ("tensor", "dp"), None),
        P(None, None, ("tensor", "dp")),
        P(None, ("tensor", "dp")),
        P(None, None, ("dp", "tensor")),
        P(None, None, ("dp", "tensor")),
    )
    out_specs = (
        P(("dp", "tensor"), None),
        P(("dp", "tensor"), None),
        P(None, "dp", "tensor"),
        P(None, "dp", "tensor"),
        P(None, "dp", "tensor"),
        P(None, ("tensor", "dp"), None),
        P(None, "dp", "tensor"),
        P(None, ("tensor", "dp"), None),
        P(None, None, ("tensor", "dp")),
        P(None, ("tensor", "dp")),
        P(None, None, ("dp", "tensor")),
        P(None, None, ("dp", "tensor")),
    )
    return jax.shard_map(
        on_device, mesh=mesh, in_specs=in_specs, out_specs=out_specs, check_vma=False
    )
```

profile of v0, /device:TPU:0, one launch (start us, length us, event | category | flops | bytes accessed | tf_op | source)
XLA Modules:
  0.0 2644.9 jit_solution(14100116275496108922)
XLA Ops:
  15.2 23.8 all-gather.1
  43.0 31.3 %all-gather.61.cloned.1.call-done = bf16[1,1024,512]{2,1,0:T(8,128)(2,1)} async-done(((bf16[1,64,512]{2,1,0:T(8,128)(2,1)}), bf16[1,1024,512]{2,1,0:T(8,128)(2,1)}) %all-gather.61.cloned.1.call-update) | async-done | bytes 1048592 | tf_op jit(solution)/shard_map/all_gather | solution.py:228
  76.6 37.3 %all-gather.59.cloned.1.call-done = bf16[1,1024,512]{2,1,0:T(8,128)(2,1)} async-done(((bf16[1,64,512]{2,1,0:T(8,128)(2,1)}), bf16[1,1024,512]{2,1,0:T(8,128)(2,1)}) %all-gather.59.cloned.1.call-update) | async-done | bytes 1048592 | tf_op jit(solution)/shard_map/all_gather | solution.py:227
  121.0 32.4 %all-gather.57.cloned.1.call-done = bf16[1,1024,512]{2,1,0:T(8,128)(2,1)} async-done(((bf16[1,64,512]{2,1,0:T(8,128)(2,1)}), bf16[1,1024,512]{2,1,0:T(8,128)(2,1)}) %all-gather.57.cloned.1.call-update) | async-done | bytes 1048592 | tf_op jit(solution)/shard_map/all_gather | solution.py:229
  161.8 31.1 %all-gather.63.cloned.1.call-done = bf16[1,512,1024]{2,1,0:T(8,128)(2,1)} async-done(((bf16[1,32,1024]{2,1,0:T(8,128)(2,1)}), bf16[1,512,1024]{2,1,0:T(8,128)(2,1)}) %all-gather.63.cloned.1.call-update) | async-done | bytes 1048592 | tf_op jit(solution)/shard_map/all_gather | solution.py:230
  196.1 69.7 %all-gather.6 = f32[1,2,1024]{1,0,2:T(1,128)S(1)} all-gather(f32[1,2,32]{1,0,2:T(1,128)S(1)} %copy.113), channel_id=8, replica_groups=mesh['dp'=16,'tensor'=2] {'dp','tensor'}, dimensions={2}, use_global_device_ids=true | all-gather | bytes 8448 | tf_op jit(solution)/shard_map/all_gather | solution.py:237
  265.8 66.4 %all-gather.5 = f32[1,4,1024]{1,0,2:T(1,128)S(1)} all-gather(f32[1,4,32]{1,0,2:T(1,128)S(1)} %copy.112), channel_id=7, replica_groups=mesh['dp'=16,'tensor'=2] {'dp','tensor'}, dimensions={2}, use_global_device_ids=true | all-gather | bytes 16896 | tf_op jit(solution)/shard_map/all_gather | solution.py:238
  338.4 21.7 slice_reduce_fusion.6
  367.0 17.4 all-gather.8
  384.6 53.6 %all-gather.65.cloned.1.call-done = bf16[1,1024,2048]{2,1,0:T(8,128)(2,1)} async-done(((bf16[1,64,2048]{2,1,0:T(8,128)(2,1)}), bf16[1,1024,2048]{2,1,0:T(8,128)(2,1)}) %all-gather.65.cloned.1.call-update) | async-done | bytes 4194320 | tf_op jit(solution)/shard_map/all_gather | solution.py:231
  453.0 37.3 %all-gather.67.cloned.1.call-done = bf16[1,2048,1024]{2,1,0:T(8,128)(2,1)} async-done(((bf16[1,128,1024]{2,1,0:T(8,128)(2,1)}), bf16[1,2048,1024]{2,1,0:T(8,128)(2,1)}) %all-gather.67.cloned.1.call-update) | async-done | bytes 4194320 | tf_op jit(solution)/shard_map/all_gather | solution.py:232
  496.6 18.2 reduce-scatter.53.cloned.1.call-done
  519.8 22.4 all-gather.11
  555.0 22.2 all-gather.45.cloned.1.call-done
  579.5 38.4 %all-gather.71.cloned.1.call-done = bf16[1,1024,512]{2,1,0:T(8,128)(2,1)} async-done(((bf16[1,64,512]{2,1,0:T(8,128)(2,1)}), bf16[1,1024,512]{2,1,0:T(8,128)(2,1)}) %all-gather.71.cloned.1.call-update) | async-done | bytes 1048592 | tf_op jit(solution)/shard_map/all_gather | solution.py:227
  625.0 32.4 %all-gather.69.cloned.1.call-done = bf16[1,1024,512]{2,1,0:T(8,128)(2,1)} async-done(((bf16[1,64,512]{2,1,0:T(8,128)(2,1)}), bf16[1,1024,512]{2,1,0:T(8,128)(2,1)}) %all-gather.69.cloned.1.call-update) | async-done | bytes 1048592 | tf_op jit(solution)/shard_map/all_gather | solution.py:229
  666.1 30.2 %all-gather.75.cloned.1.call-done = bf16[1,512,1024]{2,1,0:T(8,128)(2,1)} async-done(((bf16[1,32,1024]{2,1,0:T(8,128)(2,1)}), bf16[1,512,1024]{2,1,0:T(8,128)(2,1)}) %all-gather.75.cloned.1.call-update) | async-done | bytes 1048592 | tf_op jit(solution)/shard_map/all_gather | solution.py:230
  700.1 71.1 %all-gather.16 = f32[1,2,1024]{1,0,2:T(1,128)S(1)} all-gather(f32[1,2,32]{1,0,2:T(1,128)S(1)} %copy.116), channel_id=18, replica_groups=mesh['dp'=16,'tensor'=2] {'dp','tensor'}, dimensions={2}, use_global_device_ids=true | all-gather | bytes 8448 | tf_op jit(solution)/shard_map/all_gather | solution.py:237
  771.2 66.6 %all-gather.15 = f32[1,4,1024]{1,0,2:T(1,128)S(1)} all-gather(f32[1,4,32]{1,0,2:T(1,128)S(1)} %copy.115), channel_id=17, replica_groups=mesh['dp'=16,'tensor'=2] {'dp','tensor'}, dimensions={2}, use_global_device_ids=true | all-gather | bytes 16896 | tf_op jit(solution)/shard_map/all_gather | solution.py:238
  844.0 21.7 slice_reduce_fusion
  903.4 38.4 %all-gather.79.cloned.1.call-done = bf16[1,2048,1024]{2,1,0:T(8,128)(2,1)} async-done(((bf16[1,128,1024]{2,1,0:T(8,128)(2,1)}), bf16[1,2048,1024]{2,1,0:T(8,128)(2,1)}) %all-gather.79.cloned.1.call-update) | async-done | bytes 4194320 | tf_op jit(solution)/shard_map/all_gather | solution.py:232
  947.9 18.9 reduce-scatter.57.cloned.1.call-done
  973.6 21.4 all-gather.49.cloned.1.call-done
  1008.5 20.4 reduce-scatter.59.cloned.1.call-done
  1035.2 21.0 all-gather.51.cloned.1.call-done
  1076.0 20.4 reduce-scatter.61.cloned.1.call-done
  1101.2 21.2 all-gather.53.cloned.1.call-done
  1136.0 20.4 reduce-scatter.63.cloned.1.call-done
  1262.2 56.5 %reduce-scatter.97.cloned.1.call-done = f32[32,2]{1,0:T(8,128)} async-done(((f32[1024,2]{1,0:T(8,128)}), f32[32,2]{1,0:T(8,128)}) %reduce-scatter.97.cloned.1.call-update) | async-done | bytes 272
  1319.5 54.3 %reduce-scatter.93.cloned.1.call-done = bf16[32,2]{1,0:T(8,128)(2,1)} async-done(((bf16[512,2]{1,0:T(8,128)(2,1)}), bf16[32,2]{1,0:T(8,128)(2,1)}) %reduce-scatter.93.cloned.1.call-update) | async-done | bytes 144
  1374.6 59.8 %reduce-scatter.81.cloned.1.call-done = bf16[64,512]{1,0:T(8,128)(2,1)} async-done(((bf16[1024,512]{1,0:T(8,128)(2,1)}), bf16[64,512]{1,0:T(8,128)(2,1)}) %reduce-scatter.81.cloned.1.call-update) | async-done | bytes 65552
  1435.3 59.5 %reduce-scatter.85.cloned.1.call-done = bf16[64,512]{1,0:T(8,128)(2,1)} async-done(((bf16[1024,512]{1,0:T(8,128)(2,1)}), bf16[64,512]{1,0:T(8,128)(2,1)}) %reduce-scatter.85.cloned.1.call-update) | async-done | bytes 65552
  1495.8 59.1 %reduce-scatter.89.cloned.1.call-done = bf16[64,512]{1,0:T(8,128)(2,1)} async-done(((bf16[1024,512]{1,0:T(8,128)(2,1)}), bf16[64,512]{1,0:T(8,128)(2,1)}) %reduce-scatter.89.cloned.1.call-update) | async-done | bytes 65552
  1555.9 133.9 %reduce-scatter.101.cloned.1.call-done = f32[32,4]{1,0:T(8,128)} async-done(((f32[1024,4]{1,0:T(8,128)}), f32[32,4]{1,0:T(8,128)}) %reduce-scatter.101.cloned.1.call-update) | async-done | bytes 528
  1690.6 30.0 %all-reduce.2 = (bf16[2048]{0:T(1024)(128)(2,1)S(1)}, bf16[2048]{0:T(1024)(128)(2,1)S(1)}) all-reduce(bf16[2048]{0:T(1024)(128)(2,1)S(1)} %get-tuple-element.242, bf16[2048]{0:T(1024)(128)(2,1)S(1)} %get-tuple-element.244), channel_id=45, replica_groups=mesh['dp'=16,'tensor'=2] {'dp'}, use_global_device_ids=true, to_apply=%region_51.52.clone | all-reduce | flops 4096 | bytes 16384
  1721.3 100.8 %reduce-scatter.95.cloned.1.call-done = f32[32,2]{1,0:T(8,128)} async-done(((f32[1024,2]{1,0:T(8,128)}), f32[32,2]{1,0:T(8,128)}) %reduce-scatter.95.cloned.1.call-update) | async-done | bytes 272
  1823.4 130.9 %reduce-scatter.99.cloned.1.call-done = f32[32,4]{1,0:T(8,128)} async-done(((f32[1024,4]{1,0:T(8,128)}), f32[32,4]{1,0:T(8,128)}) %reduce-scatter.99.cloned.1.call-update) | async-done | bytes 528
  1955.8 53.5 %reduce-scatter.91.cloned.1.call-done = bf16[32,2]{1,0:T(8,128)(2,1)} async-done(((bf16[512,2]{1,0:T(8,128)(2,1)}), bf16[32,2]{1,0:T(8,128)(2,1)}) %reduce-scatter.91.cloned.1.call-update) | async-done | bytes 144
  2010.6 59.1 %reduce-scatter.79.cloned.1.call-done = bf16[64,512]{1,0:T(8,128)(2,1)} async-done(((bf16[1024,512]{1,0:T(8,128)(2,1)}), bf16[64,512]{1,0:T(8,128)(2,1)}) %reduce-scatter.79.cloned.1.call-update) | async-done | bytes 65552
  2071.7 58.5 %reduce-scatter.83.cloned.1.call-done = bf16[64,512]{1,0:T(8,128)(2,1)} async-done(((bf16[1024,512]{1,0:T(8,128)(2,1)}), bf16[64,512]{1,0:T(8,128)(2,1)}) %reduce-scatter.83.cloned.1.call-update) | async-done | bytes 65552
  2132.1 58.1 %reduce-scatter.87.cloned.1.call-done = bf16[64,512]{1,0:T(8,128)(2,1)} async-done(((bf16[1024,512]{1,0:T(8,128)(2,1)}), bf16[64,512]{1,0:T(8,128)(2,1)}) %reduce-scatter.87.cloned.1.call-update) | async-done | bytes 65552
  2192.2 58.6 %reduce-scatter.69.cloned.1.call-done = bf16[32,1024]{1,0:T(8,128)(2,1)} async-done(((bf16[512,1024]{1,0:T(8,128)(2,1)}), bf16[32,1024]{1,0:T(8,128)(2,1)}) %reduce-scatter.69.cloned.1.call-update) | async-done | bytes 65552 | tf_op jit(solution)/shard_map/reduce_scatter | solution.py:272
  2250.8 60.1 %reduce-scatter.67.cloned.1.call-done = bf16[32,1024]{1,0:T(8,128)(2,1)} async-done(((bf16[512,1024]{1,0:T(8,128)(2,1)}), bf16[32,1024]{1,0:T(8,128)(2,1)}) %reduce-scatter.67.cloned.1.call-update) | async-done | bytes 65552 | tf_op jit(solution)/shard_map/reduce_scatter | solution.py:272
  2312.4 20.7 reduce-scatter.65.cloned.1.call-done
  2335.3 73.9 %reduce-scatter.73.cloned.1.call-done = bf16[64,2048]{1,0:T(8,128)(2,1)} async-done(((bf16[1024,2048]{1,0:T(8,128)(2,1)}), bf16[64,2048]{1,0:T(8,128)(2,1)}) %reduce-scatter.73.cloned.1.call-update) | async-done | bytes 262160 | tf_op jit(solution)/shard_map/reduce_scatter | solution.py:275
  2409.2 75.9 %reduce-scatter.71.cloned.1.call-done = bf16[64,2048]{1,0:T(8,128)(2,1)} async-done(((bf16[1024,2048]{1,0:T(8,128)(2,1)}), bf16[64,2048]{1,0:T(8,128)(2,1)}) %reduce-scatter.71.cloned.1.call-update) | async-done | bytes 262160 | tf_op jit(solution)/shard_map/reduce_scatter | solution.py:275
  2487.2 73.1 %reduce-scatter.77.cloned.1.call-done = bf16[128,1024]{1,0:T(8,128)(2,1)} async-done(((bf16[2048,1024]{1,0:T(8,128)(2,1)}), bf16[128,1024]{1,0:T(8,128)(2,1)}) %reduce-scatter.77.cloned.1.call-update) | async-done | bytes 262160 | tf_op jit(solution)/shard_map/reduce_scatter | solution.py:278
  2560.3 75.6 %reduce-scatter.75.cloned.1.call-done = bf16[128,1024]{1,0:T(8,128)(2,1)} async-done(((bf16[2048,1024]{1,0:T(8,128)(2,1)}), bf16[128,1024]{1,0:T(8,128)(2,1)}) %reduce-scatter.75.cloned.1.call-update) | async-done | bytes 262160 | tf_op jit(solution)/shard_map/reduce_scatter | solution.py:278
  (380 shorter events, 348.9 us)
Async XLA Ops:
  7.2 35.8 %all-gather.41.cloned.1.call-start = ((), (), s32[]{:S(2)}) async-start(), calls=%async_computation.26 | async-start | bytes 1572864 | tf_op jit(solution)/shard_map/all_gather | solution.py:38
  7.9 66.4 %all-gather.61.cloned.1.call-start = ((), (), s32[]{:S(2)}) async-start(), calls=%async_computation.50 | async-start | bytes 1114112 | tf_op jit(solution)/shard_map/all_gather | solution.py:228
  9.5 104.4 %all-gather.59.cloned.1.call-start = ((), (), s32[]{:S(2)}) async-start(), calls=%async_computation.49 | async-start | bytes 1114112 | tf_op jit(solution)/shard_map/all_gather | solution.py:227
  11.1 142.3 %all-gather.57.cloned.1.call-start = ((), (), s32[]{:S(2)}) async-start(), calls=%async_computation.48 | async-start | bytes 1114112 | tf_op jit(solution)/shard_map/all_gather | solution.py:229
  12.7 180.2 %all-gather.63.cloned.1.call-start = ((), (), s32[]{:S(2)}) async-start(), calls=%async_computation.51 | async-start | bytes 1114112 | tf_op jit(solution)/shard_map/all_gather | solution.py:230
  14.3 345.9 %reduce-scatter.51.cloned.1.call-start = ((), (), s32[]{:S(2)}) async-start(), calls=%async_computation.27 | async-start | bytes 1572864 | tf_op jit(solution)/shard_map/reduce_scatter | solution.py:46
  161.8 198.4 %copy-start.3 = (bf16[256,1024]{1,0:T(8,128)(2,1)S(1)}, bf16[256,1024]{1,0:T(8,128)(2,1)}, u32[]{:S(2)}) copy-start(bf16[256,1024]{1,0:T(8,128)(2,1)} %param.13) | copy-start | bytes 1572868
  195.8 188.8 %all-gather.43.cloned.1.call-start = ((), (), s32[]{:S(2)}) async-start(), calls=%async_computation.28 | async-start | bytes 1572864 | tf_op jit(solution)/shard_map/all_gather | solution.py:38
  196.1 169.0 %copy-start.27 = (bf16[2,64,2048]{2,1,0:T(8,128)(2,1)S(1)}, bf16[2,64,2048]{2,1,0:T(8,128)(2,1)}, u32[]{:S(2)}) copy-start(bf16[2,64,2048]{2,1,0:T(8,128)(2,1)} %param.20) | copy-start | bytes 1572868
  365.1 73.1 %all-gather.65.cloned.1.call-start = ((), (), s32[]{:S(2)}) async-start(), calls=%async_computation.52 | async-start | bytes 4456448 | tf_op jit(solution)/shard_map/all_gather | solution.py:231
  366.0 124.2 %all-gather.67.cloned.1.call-start = ((), (), s32[]{:S(2)}) async-start(), calls=%async_computation.53 | async-start | bytes 4456448 | tf_op jit(solution)/shard_map/all_gather | solution.py:232
  366.9 147.9 %reduce-scatter.53.cloned.1.call-start = ((), (), s32[]{:S(2)}) async-start(), calls=%async_computation.29 | async-start | bytes 1572864 | tf_op jit(solution)/shard_map/reduce_scatter | solution.py:46
  495.8 59.2 %all-gather.73.cloned.1.call-start = ((), (), s32[]{:S(2)}) async-start(), calls=%async_computation.56 | async-start | bytes 1114112 | tf_op jit(solution)/shard_map/all_gather | solution.py:228
  496.6 80.7 %all-gather.45.cloned.1.call-start = ((), (), s32[]{:S(2)}) async-start(), calls=%async_computation.30 | async-start | bytes 1572864 | tf_op jit(solution)/shard_map/all_gather | solution.py:38
  517.7 100.2 %all-gather.71.cloned.1.call-start = ((), (), s32[]{:S(2)}) async-start(), calls=%async_computation.55 | async-start | bytes 1114112 | tf_op jit(solution)/shard_map/all_gather | solution.py:227
  518.5 138.9 %all-gather.69.cloned.1.call-start = ((), (), s32[]{:S(2)}) async-start(), calls=%async_computation.54 | async-start | bytes 1114112 | tf_op jit(solution)/shard_map/all_gather | solution.py:229
  519.1 177.3 %all-gather.75.cloned.1.call-start = ((), (), s32[]{:S(2)}) async-start(), calls=%async_computation.57 | async-start | bytes 1114112 | tf_op jit(solution)/shard_map/all_gather | solution.py:230
  519.6 346.1 %reduce-scatter.55.cloned.1.call-start = ((), (), s32[]{:S(2)}) async-start(), calls=%async_computation.31 | async-start | bytes 1572864 | tf_op jit(solution)/shard_map/reduce_scatter | solution.py:46
  699.3 187.4 %all-gather.77.cloned.1.call-start = ((), (), s32[]{:S(2)}) async-start(), calls=%async_computation.58 | async-start | bytes 4456448 | tf_op jit(solution)/shard_map/all_gather | solution.py:231
  699.9 188.3 %all-gather.47.cloned.1.call-start = ((), (), s32[]{:S(2)}) async-start(), calls=%async_computation.32 | async-start | bytes 1572864 | tf_op jit(solution)/shard_map/all_gather | solution.py:38
  868.7 73.1 %all-gather.79.cloned.1.call-start = ((), (), s32[]{:S(2)}) async-start(), calls=%async_computation.59 | async-start | bytes 4456448 | tf_op jit(solution)/shard_map/all_gather | solution.py:232
  869.4 97.4 %reduce-scatter.57.cloned.1.call-start = ((), (), s32[]{:S(2)}) async-start(), calls=%async_computation.33 | async-start | bytes 1572864 | tf_op jit(solution)/shard_map/reduce_scatter | solution.py:46
  947.9 47.1 %all-gather.49.cloned.1.call-start = ((), (), s32[]{:S(2)}) async-start(), calls=%async_computation.34 | async-start | bytes 1572864 | tf_op jit(solution)/shard_map/all_gather | solution.py:42
  973.5 55.4 %reduce-scatter.59.cloned.1.call-start = ((), (), s32[]{:S(2)}) async-start(), calls=%async_computation.35 | async-start | bytes 1572864 | tf_op jit(solution)/shard_map/reduce_scatter | solution.py:55
  1008.4 47.8 %all-gather.51.cloned.1.call-start = ((), (), s32[]{:S(2)}) async-start(), calls=%async_computation.36 | async-start | bytes 1572864 | tf_op jit(solution)/shard_map/all_gather | solution.py:42
  1034.8 61.7 %reduce-scatter.61.cloned.1.call-start = ((), (), s32[]{:S(2)}) async-start(), calls=%async_computation.37 | async-start | bytes 1572864 | tf_op jit(solution)/shard_map/reduce_scatter | solution.py:55
  1076.0 46.5 %all-gather.53.cloned.1.call-start = ((), (), s32[]{:S(2)}) async-start(), calls=%async_computation.38 | async-start | bytes 1572864 | tf_op jit(solution)/shard_map/all_gather | solution.py:42
  1101.0 55.5 %reduce-scatter.63.cloned.1.call-start = ((), (), s32[]{:S(2)}) async-start(), calls=%async_computation.39 | async-start | bytes 1572864 | tf_op jit(solution)/shard_map/reduce_scatter | solution.py:55
  1136.0 46.4 %all-gather.55.cloned.1.call-start = ((), (), s32[]{:S(2)}) async-start(), calls=%async_computation.40 | async-start | bytes 1572864 | tf_op jit(solution)/shard_map/all_gather | solution.py:42
  1160.9 157.8 %reduce-scatter.97.cloned.1.call-start = ((), (), s32[]{:S(2)}) async-start(), calls=%async_computation.69 | async-start | bytes 540672
  1162.0 211.8 %reduce-scatter.93.cloned.1.call-start = ((), (), s32[]{:S(2)}) async-start(), calls=%async_computation.67 | async-start | bytes 139264
  1163.1 271.2 %reduce-scatter.81.cloned.1.call-start = ((), (), s32[]{:S(2)}) async-start(), calls=%async_computation.61 | async-start | bytes 1114112
  1166.3 328.5 %reduce-scatter.85.cloned.1.call-start = ((), (), s32[]{:S(2)}) async-start(), calls=%async_computation.63 | async-start | bytes 1114112
  1168.1 386.8 %reduce-scatter.89.cloned.1.call-start = ((), (), s32[]{:S(2)}) async-start(), calls=%async_computation.65 | async-start | bytes 1114112
  1170.0 519.8 %reduce-scatter.101.cloned.1.call-start = ((), (), s32[]{:S(2)}) async-start(), calls=%async_computation.71 | async-start | bytes 540672
  1171.1 651.0 %reduce-scatter.95.cloned.1.call-start = ((), (), s32[]{:S(2)}) async-start(), calls=%async_computation.68 | async-start | bytes 540672
  1172.2 782.1 %reduce-scatter.99.cloned.1.call-start = ((), (), s32[]{:S(2)}) async-start(), calls=%async_computation.70 | async-start | bytes 540672
  1173.4 835.9 %reduce-scatter.91.cloned.1.call-start = ((), (), s32[]{:S(2)}) async-start(), calls=%async_computation.66 | async-start | bytes 139264
  1202.7 867.0 %reduce-scatter.79.cloned.1.call-start = ((), (), s32[]{:S(2)}) async-start(), calls=%async_computation.60 | async-start | bytes 1114112
  1206.1 924.1 %reduce-scatter.83.cloned.1.call-start = ((), (), s32[]{:S(2)}) async-start(), calls=%async_computation.62 | async-start | bytes 1114112
  1213.9 976.4 %reduce-scatter.87.cloned.1.call-start = ((), (), s32[]{:S(2)}) async-start(), calls=%async_computation.64 | async-start | bytes 1114112
  1219.2 1031.5 %reduce-scatter.69.cloned.1.call-start = ((), (), s32[]{:S(2)}) async-start(), calls=%async_computation.43 | async-start | bytes 1114112 | tf_op jit(solution)/shard_map/reduce_scatter | solution.py:272
  1222.4 1088.4 %reduce-scatter.67.cloned.1.call-start = ((), (), s32[]{:S(2)}) async-start(), calls=%async_computation.42 | async-start | bytes 1114112 | tf_op jit(solution)/shard_map/reduce_scatter | solution.py:272
  1225.4 1107.7 %reduce-scatter.65.cloned.1.call-start = ((), (), s32[]{:S(2)}) async-start(), calls=%async_computation.41 | async-start | bytes 1572864 | tf_op jit(solution)/shard_map/reduce_scatter | solution.py:55
  1232.8 1176.4 %reduce-scatter.73.cloned.1.call-start = ((), (), s32[]{:S(2)}) async-start(), calls=%async_computation.45 | async-start | bytes 4456448 | tf_op jit(solution)/shard_map/reduce_scatter | solution.py:275
  1238.8 1246.3 %reduce-scatter.71.cloned.1.call-start = ((), (), s32[]{:S(2)}) async-start(), calls=%async_computation.44 | async-start | bytes 4456448 | tf_op jit(solution)/shard_map/reduce_scatter | solution.py:275
  1246.0 1314.3 %reduce-scatter.77.cloned.1.call-start = ((), (), s32[]{:S(2)}) async-start(), calls=%async_computation.47 | async-start | bytes 4456448 | tf_op jit(solution)/shard_map/reduce_scatter | solution.py:278
  1253.2 1382.7 %reduce-scatter.75.cloned.1.call-start = ((), (), s32[]{:S(2)}) async-start(), calls=%async_computation.46 | async-start | bytes 4456448 | tf_op jit(solution)/shard_map/reduce_scatter | solution.py:278
  (55 other events, 651.4 us)
Sparse Core Ops, SparseCore 0:
  9.6 23.9 all-gather.40
  36.3 37.9 all-gather.60
  77.0 36.8 all-gather.58
  116.5 36.8 all-gather.56
  156.0 36.8 all-gather.62
  196.0 21.6 reduce-scatter.50
  365.2 19.3 all-gather.42
  387.6 50.5 all-gather.64
  441.1 49.0 all-gather.66
  495.9 18.7 reduce-scatter.52
  516.9 38.0 all-gather.72
  557.0 20.2 all-gather.44
  580.0 37.9 all-gather.70
  620.5 36.8 all-gather.68
  659.4 36.8 all-gather.74
  699.4 21.6 reduce-scatter.54
  723.9 51.7 all-gather.76
  868.8 19.3 all-gather.46
  891.1 50.5 all-gather.78
  948.0 18.7 reduce-scatter.56
  973.6 21.3 all-gather.48
  1008.6 20.3 reduce-scatter.58
  1034.9 21.2 all-gather.50
  1076.1 20.3 reduce-scatter.60
  1101.1 21.2 all-gather.52
  1136.1 20.3 reduce-scatter.62
  1161.0 21.2 all-gather.54
  1184.7 133.9 reduce-scatter.96
  1322.8 50.9 reduce-scatter.92
  1377.8 56.4 reduce-scatter.80
  1438.4 56.3 reduce-scatter.84
  1498.4 56.4 reduce-scatter.88
  1557.1 132.6 reduce-scatter.100
  1692.0 129.9 reduce-scatter.94
  1824.4 129.9 reduce-scatter.98
  1958.2 50.9 reduce-scatter.90
  2013.3 56.4 reduce-scatter.78
  2073.8 56.2 reduce-scatter.82
  2133.6 56.5 reduce-scatter.86
  2194.3 56.4 reduce-scatter.68
  2254.4 56.4 reduce-scatter.66
  2313.8 19.2 reduce-scatter.64
  2336.8 72.3 reduce-scatter.72
  2413.5 71.5 reduce-scatter.70
  2488.8 71.4 reduce-scatter.76
  2564.5 71.3 reduce-scatter.74
where the time goes:
time: 2660 us; the launch traced here: 2640 us
  waiting for transfers between devices  1890 us (71%)
  blocking collectives  385 us (14%)
  matrix products  183 us (7%)
  local copies, waits for them, and re-layouts  108 us (4%)
  other arithmetic  56.4 us (2%)
    unnamed x58, waiting for transfers between devices  889 us
    reduce_scatter x2, waiting for transfers between devices, on_device(): lax.psum_scatter(g_u.astype(jnp.bfloat16), 'dp', scatter_dimension=0, til...  150 us
    reduce_scatter x2, waiting for transfers between devices, on_device(): lax.psum_scatter(g_d.astype(jnp.bfloat16), 'dp', scatter_dimension=0, til...  149 us
    all_gather x2, blocking collectives, on_device(): lax.all_gather(norm_gain[layer], ('dp', 'tensor'), axis=1, tiled=True)  141 us
    all_gather x2, blocking collectives, on_device(): lax.all_gather(shift_bias[layer], ('dp', 'tensor'), axis=1, tiled=True)  133 us
    reduce_scatter x2, waiting for transfers between devices, on_device(): lax.psum_scatter(g_o.astype(jnp.bfloat16), 'dp', scatter_dimension=0, til...  119 us
    reduce_scatter x4, waiting for transfers between devices, sum_grads(): lax.psum_scatter(term(jnp.int32(0), lax.axis_size('tensor') * rows).astyp...  81.9 us
    all_gather x2, waiting for transfers between devices, on_device(): lax.all_gather(w_query[layer], 'dp', axis=0, tiled=True)  75.7 us
  transfers between devices with their start and end apart: 46, of which 42 were waited for; matrix products, arithmetic and copies ran while one was open for 9% of the time, Pallas kernels for 0%

commit v1 on v0

--- a/solution.py
+++ b/solution.py
@@ -1,6 +1,11 @@
+import functools
+import math
+
 import jax
 import jax.numpy as jnp
 from jax import lax
+from jax.experimental import pallas as pl
+from jax.experimental.pallas import tpu as pltpu
 from jax.sharding import PartitionSpec as P
 
 HEAD = 64
@@ -139,7 +144,7 @@
     return (result, kept)
 
 
-def backward_layer(grad, mats, vecs, kept, segs, seq):
+def backward_layer_any(grad, mats, vecs, kept, segs, seq):
     w_q, w_k, w_v, w_o, w_u, w_d, qvb, upb = mats
     gains, shifts = vecs
     x_rows, query, key, value, attended, totals, mixed, n_rows, pre, hidden, second = kept
@@ -199,7 +204,568 @@
     return (d_stream, mat_grads, vec_grads)
 
 
+def backward_layer(grad, mats, vecs, kept, segs, seq):
+    w_q, w_k, w_v, w_o, w_u, w_d, qvb, upb = mats
+    gains, shifts = vecs
+    x_rows, query, key, value, attended, totals, mixed, n_rows, pre, hidden, second = kept
+    seqs = segs.shape[0]
+    rows = grad.shape[0]
+    width = query.shape[1]
+    local_heads = width // HEAD
+
+    def split(matrix):
+        return matrix.reshape(seqs, seq, local_heads, HEAD)
+
+    _, pull_second = jax.vjp(layer_norm, second, gains[1], shifts[3])
+    d_second, d_gain_two, d_shift_two = pull_second(grad)
+    d_down_bias = jnp.sum(d_second, axis=0)
+    d_f = gather_grads(d_second.astype(jnp.bfloat16))
+    grad_down = inner(hidden, d_f)
+    d_hidden = times_back(d_f, w_d)
+    d_pre = (d_hidden * pre.astype(jnp.float32)).astype(jnp.bfloat16)
+    grad_up = inner(n_rows, d_pre)
+    d_up_bias = jnp.sum(d_pre.astype(jnp.float32), axis=0)
+
+    def up_term(start, count):
+        return times_back(d_pre, w_u)
+
+    d_normed = d_second + sum_grads(up_term, rows)
+    _, pull_first = jax.vjp(layer_norm, mixed, gains[0], shifts[1])
+    d_mixed, d_gain_one, d_shift_one = pull_first(d_normed)
+    d_out_bias = jnp.sum(d_mixed, axis=0)
+    d_a = gather_grads(d_mixed.astype(jnp.bfloat16))
+    grad_out = inner(attended, d_a)
+    d_att = times_back(d_a, w_o).astype(jnp.bfloat16)
+    d_query, d_key, d_value = lax.map(
+        attend_back, (split(query), split(key), split(value), segs, totals, split(d_att))
+    )
+    d_query = d_query.reshape(seqs * seq, width)
+    d_key = d_key.reshape(seqs * seq, width)
+    d_value = d_value.reshape(seqs * seq, width)
+    grad_q = inner(x_rows, d_query)
+    grad_k = inner(x_rows, d_key)
+    grad_v = inner(x_rows, d_value)
+    d_qv = jnp.stack(
+        [jnp.sum(d_query.astype(jnp.float32), axis=0), jnp.sum(d_value.astype(jnp.float32), axis=0)]
+    )
+
+    def in_term(start, count):
+        part = times_back(d_query, w_q)
+        part = part + times_back(d_key, w_k)
+        return part + times_back(d_value, w_v)
+
+    d_stream = d_mixed + sum_grads(in_term, rows)
+    mat_grads = (grad_q, grad_k, grad_v, grad_out, grad_up, grad_down, d_qv, d_up_bias)
+    vec_grads = (
+        jnp.stack([d_gain_one, d_gain_two]),
+        jnp.stack([d_out_bias, d_shift_one, d_down_bias, d_shift_two]),
+    )
+    return (d_stream, mat_grads, vec_grads)
+
+
+MESH = pl.DeviceIdType.MESH
+BF = jnp.bfloat16
+F32 = jnp.float32
+CH = 12
+
+
+def nt(left, right):
+    return lax.dot_general(left, right, (((1,), (1,)), ((), ())), preferred_element_type=F32)
+
+
+def nn(left, right):
+    return lax.dot_general(left, right, (((1,), (0,)), ((), ())), preferred_element_type=F32)
+
+
+def tn(left, right):
+    return lax.dot_general(left, right, (((0,), (0,)), ((), ())), preferred_element_type=F32)
+
+
+def remote(src, dst, send_sem, recv_sem, device):
+    return pltpu.make_async_remote_copy(
+        src_ref=src, dst_ref=dst, send_sem=send_sem, recv_sem=recv_sem, device_id=device, device_id_type=MESH
+    )
+
+
+class Place:
+    def __init__(self, depth):
+        self.depth = depth
+        self.dp = lax.axis_index("dp")
+        self.x = lax.axis_index("tensor")
+        self.z = self.dp // 4
+        self.y = (self.dp // 2) % 2
+        self.c = self.dp % 2
+
+    def at(self, z, y, c):
+        return {"dp": z * 4 + y * 2 + c, "tensor": self.x}
+
+    def far(self, step):
+        return self.at((self.z + step) % self.depth, self.y, self.c)
+
+    def before(self, step):
+        return (self.z + self.depth - step) % self.depth
+
+    @property
+    def side(self):
+        return self.at(self.z, 1 - self.y, self.c)
+
+    @property
+    def twin(self):
+        return self.at(self.z, self.y, 1 - self.c)
+
+    @property
+    def peer(self):
+        return {"dp": self.dp, "tensor": 1 - self.x}
+
+    def greet(self):
+        barrier = pltpu.get_barrier_semaphore()
+        partners = [self.far(i) for i in range(1, self.depth)] + [self.side, self.twin, self.peer]
+        for device in partners:
+            pl.semaphore_signal(barrier, inc=1, device_id=device, device_id_type=MESH)
+        pl.semaphore_wait(barrier, len(partners))
+
+
+class Gather:
+    def __init__(self, place, wp, wg, send, recv, total):
+        self.p, self.wp, self.wg, self.send, self.recv, self.total = place, wp, wg, send, recv, total
+        self.view = wg.reshape(wg.shape[0], place.depth, 2, 2, *wg.shape[2:])
+        self.time = 0
+        self.have = 0
+
+    def far(self, k, i):
+        p = self.p
+        return remote(self.wp.at[k], self.wg.at[k, p.dp], self.send.at[k, i - 1], self.recv.at[k, i - 1], p.far(i))
+
+    def far_in(self, k, i):
+        p = self.p
+        ref = self.wg.at[k, p.before(i) * 4 + p.y * 2 + p.c]
+        return remote(ref, ref, self.send.at[k, i - 1], self.recv.at[k, i - 1], p.far(i))
+
+    def side(self, k, y):
+        p, d = self.p, self.p.depth - 1
+        ref = self.view.at[k, :, y, p.c]
+        return remote(ref, ref, self.send.at[k, d], self.recv.at[k, d], p.side)
+
+    def twin(self, k, c):
+        p, d = self.p, self.p.depth
+        ref = self.view.at[k, :, :, c]
+        return remote(ref, ref, self.send.at[k, d], self.recv.at[k, d], p.twin)
+
+    def begin(self, ahead):
+        self.ahead = ahead
+        for k in range(ahead):
+            for i in range(1, self.p.depth):
+                self.far(k, i).start()
+
+    def tick(self):
+        t, n = self.time, self.total
+        if t >= n + 3:
+            return
+        if t + self.ahead < n:
+            for i in range(1, self.p.depth):
+                self.far(t + self.ahead, i).start()
+        if t < n:
+            for i in range(1, self.p.depth):
+                self.far_in(t, i).wait_recv()
+            self.side(t, self.p.y).start()
+        if 1 <= t <= n:
+            self.side(t - 1, 1 - self.p.y).wait_recv()
+            self.twin(t - 1, self.p.c).start()
+        if t >= 2 and t - 2 < n:
+            self.twin(t - 2, 1 - self.p.c).wait_recv()
+            self.have = t - 1
+        self.time += 1
+
+    def until(self, count):
+        while self.have < count:
+            self.tick()
+
+    def finish(self):
+        self.until(self.total)
+        for k in range(self.total):
+            for i in range(1, self.p.depth):
+                self.far(k, i).wait_send()
+            self.side(k, self.p.y).wait_send()
+            self.twin(k, self.p.c).wait_send()
+
+
+def norm_rows(z, gain, shift):
+    mean = jnp.mean(z, axis=-1, keepdims=True)
+    cent = z - mean
+    var = jnp.mean(cent * cent, axis=-1, keepdims=True)
+    return cent * lax.rsqrt(var + EPS) * gain + shift
+
+
+def fwd_kernel(depth, layers, wp, vp, tok, segc, segr,
+               wg, vec_o, out_o, xg_o, qkv_o, att_o, lse_o, mix_o, ng_o, hid_o, gp_o, sec_o,
+               vg, vec, stream, normed, bias, work, prob, xg, qkv, att, lse, mix, ng, hid, gp, sec, sbuf, rbuf,
+               wqkv, wo, wu, wd,
+               w_send, w_recv, v_send, v_recv, x_send, x_recv, l_sem, o_sem, own_sem):
+    p = Place(depth)
+    x = p.x
+    rows = tok.shape[0]
+    group = 2 * rows
+    mine = pl.ds(pl.multiple_of(x * rows, rows), rows)
+    theirs = pl.ds(pl.multiple_of((1 - x) * rows, rows), rows)
+    n_chunks = layers * CH
+    gat = Gather(p, wp, wg, w_send, w_recv, n_chunks)
+    own = pltpu.make_async_copy(wp, wg.at[:, p.dp], own_sem)
+    own.start()
+    vg[x, p.z, p.y, p.c] = vp[...]
+    xg[0, mine, :] = tok[...]
+    p.greet()
+
+    def give_rows(ref, index):
+        return remote(ref, ref, x_send.at[index], x_recv.at[index], p.peer)
+
+    v_far = [remote(vg.at[x, p.z, p.y, p.c], vg.at[x, p.z, p.y, p.c], v_send.at[i - 1], v_recv.at[i - 1], p.far(i))
+             for i in range(1, depth)]
+    for copy in v_far:
+        copy.start()
+    give_rows(xg.at[0, mine, :], 0).start()
+    gat.begin(3)
+
+    stream[...] = tok[...].astype(F32)
+    def bias_rows(i, _):
+        r = pl.ds(pl.multiple_of(i * 64, 64), 64)
+        bias[r, :] = jnp.where(segc[r, :] == segr[...], 0.0, NEG)
+        return _
+    lax.fori_loop(0, group // 64, bias_rows, 0)
+
+    for copy in v_far:
+        copy.wait_recv()
+    v_side = remote(vg.at[x, :, p.y, p.c], vg.at[x, :, p.y, p.c], v_send.at[depth - 1], v_recv.at[depth - 1], p.side)
+    v_side.start()
+    v_side.wait_recv()
+    v_twin = remote(vg.at[x, :, :, p.c], vg.at[x, :, :, p.c], v_send.at[depth], v_recv.at[depth], p.twin)
+    v_twin.start()
+    own.wait()
+    v_twin.wait_recv()
+    v_peer = remote(vg.at[x], vg.at[x], v_send.at[depth + 1], v_recv.at[depth + 1], p.peer)
+    v_peer.start()
+    gat.tick()
+    v_peer.wait_recv()
+    heads_w = qkv.shape[-1]
+    for z in range(depth):
+        for y in range(2):
+            b = (z * 2 + y) * 128
+            vec[0:16, b:b + 128] = (vg[0, z, y, 0, 0:16] + vg[0, z, y, 1, 0:16]
+                                    + vg[1, z, y, 0, 0:16] + vg[1, z, y, 1, 0:16])
+    for z in range(depth):
+        for_half = vg[x, z, 0, 0, 16:24] + vg[x, z, 0, 1, 16:24] + vg[x, z, 1, 0, 16:24] + vg[x, z, 1, 1, 16:24]
+        vec[16:24, z * 128:(z + 1) * 128] = for_half
+        for y in range(2):
+            for c in range(2):
+                b = (z * 4 + y * 2 + c) * 128
+                vec[24:32, b:b + 128] = vg[x, z, y, c, 24:32]
+    outs = []
+
+    def keep(src, dst):
+        copy = pltpu.make_async_copy(src, dst, o_sem.at[len(outs)])
+        copy.start()
+        outs.append(copy)
+
+    keep(vec, vec_o)
+    loads = {}
+
+    def load(name, src, dst):
+        copy = pltpu.make_async_copy(src, dst, l_sem.at[len(loads)])
+        copy.start()
+        loads[name] = copy
+
+    def gain(l, i):
+        r = l * 2 + i
+        return vec[r:r + 1, 0:1024]
+
+    def shift(l, i):
+        r = 4 + l * 4 + i
+        return vec[r:r + 1, 0:1024]
+
+    def project(l, r):
+        for m in range(3):
+            w = wqkv[m].reshape(-1, heads_w)
+            res = nn(xg[l, r, :], w)
+            if m != 1:
+                b = 16 + l * 2 + (m // 2)
+                res = res + vec[b:b + 1, 0:heads_w]
+            qkv[l, m, r, :] = res.astype(BF)
+
+    half_lane = lax.broadcasted_iota(jnp.int32, (1, 128), 1) < HEAD
+    first_half = jnp.where(half_lane, 1.0, 0.0).astype(BF)
+    second_half = jnp.where(half_lane, 0.0, 1.0).astype(BF)
+    scale = HEAD ** -0.5
+
+    def attend(l):
+        def pair(hp, carry):
+            lanes = pl.ds(pl.multiple_of(hp * 128, 128), 128)
+            k128 = qkv[l, 1, :, lanes]
+            v_t = qkv[l, 2, :, lanes].T
+            for qb in range(group // 256):
+                q_rows = slice(qb * 256, (qb + 1) * 256)
+                q128 = qkv[l, 0, q_rows, lanes]
+                both = []
+                for half in range(2):
+                    k_half = k128 * ((second_half if half else first_half) * scale)
+                    work[half] = nt(k_half, q128)
+                    top = jnp.full((8, 256), NEG, F32)
+                    for i in range(group // 64):
+                        r = slice(i * 64, (i + 1) * 64)
+                        s = work[half, r, :] + bias[r, q_rows]
+                        work[half, r, :] = s
+                        top = jnp.maximum(top, jnp.max(s.reshape(8, 8, 256), axis=0))
+                    top = jnp.max(top, axis=0, keepdims=True)
+                    tot = jnp.zeros((8, 256), F32)
+                    for i in range(group // 64):
+                        r = slice(i * 64, (i + 1) * 64)
+                        e = jnp.exp(work[half, r, :] - top)
+                        tot = tot + jnp.sum(e.reshape(8, 8, 256), axis=0)
+                        prob[half, r, :] = e.astype(BF)
+                    tot = jnp.sum(tot, axis=0, keepdims=True)
+                    lse[l, pl.ds(hp * 2 + half, 1), q_rows] = top + jnp.log(tot)
+                    res = nn(v_t[half * HEAD:(half + 1) * HEAD], prob[half])
+                    both.append(res / tot)
+                att[l, q_rows, lanes] = jnp.concatenate(both, axis=0).T.astype(BF)
+            return carry
+        lax.fori_loop(0, heads_w // 128, pair, 0)
+
+    def out_term(l, r):
+        return nn(att[l, r, :], wo[...].reshape(heads_w, -1))
+
+    inv_sqrt2 = 2.0 ** -0.5
+    inv_sqrt_2pi = (2.0 * math.pi) ** -0.5
+
+    def up(l, j):
+        b = 24 + l
+        for cb in range(2):
+            cols = slice(j * 512 + cb * 256, j * 512 + (cb + 1) * 256)
+            w = wu[j, :, :, cb * 256:(cb + 1) * 256].reshape(-1, 256)
+            work[cb] = nn(ng[l], w) + vec[b:b + 1, cols]
+
+            def some(i, carry):
+                r = pl.ds(pl.multiple_of(i * 32, 32), 32)
+                pre = work[cb, r, :]
+                part = 0.5 + 0.5 * lax.erf(pre * inv_sqrt2)
+                hid[l, r, cols] = (pre * part).astype(BF)
+                gp[l, r, cols] = (part + pre * jnp.exp(-0.5 * pre * pre) * inv_sqrt_2pi).astype(BF)
+                return carry
+            lax.fori_loop(0, group // 32, some, 0)
+
+    def down_term(l, r, h):
+        cols = slice(h * 256, (h + 1) * 256)
+        w = wd[:, :, :, cols].reshape(-1, 256)
+        return nn(hid[l, r, :], w)
+
+    for l in range(layers):
+        c0 = l * CH
+        gat.until(c0 + 3)
+        for m in range(3):
+            load(("a", l, m), wg.at[c0 + m], wqkv.at[m])
+        gat.tick()
+        for m in range(3):
+            loads["a", l, m].wait()
+        project(l, mine)
+        give_rows(xg.at[l, theirs, :], l * 4).wait_recv()
+        keep(xg.at[l], xg_o.at[l])
+        project(l, theirs)
+        keep(qkv.at[l], qkv_o.at[l])
+        gat.tick()
+        attend(l)
+        keep(lse.at[l], lse_o.at[l])
+        keep(att.at[l], att_o.at[l])
+        gat.until(c0 + 4)
+        for hh in range(2):
+            load(("o", l, hh), wg.at[c0 + 3, :, hh * 32:(hh + 1) * 32, :], wo.at[:, :, hh * 512:(hh + 1) * 512])
+        gat.tick()
+        for hh in range(2):
+            loads["o", l, hh].wait()
+        if l > 0:
+            remote(sbuf, rbuf.at[0], x_send.at[l * 4 - 1], x_recv.at[l * 4 - 1], p.peer).wait_send()
+        sbuf[...] = out_term(l, theirs).astype(BF)
+        send = remote(sbuf, rbuf.at[l * 2], x_send.at[l * 4 + 1], x_recv.at[l * 4 + 1], p.peer)
+        send.start()
+        mix[l] = stream[...] + out_term(l, mine) + shift(l, 0)
+        gat.tick()
+        gat.tick()
+        send.wait_recv()
+        for i in range(rows // 32):
+            r = slice(i * 32, (i + 1) * 32)
+            mixed = mix[l, r, :] + rbuf[l * 2, r, :].astype(F32)
+            mix[l, r, :] = mixed
+            res = norm_rows(mixed, gain(l, 0), shift(l, 1))
+            normed[r, :] = res
+            ng[l, pl.ds(pl.multiple_of(x * rows + i * 32, 32), 32), :] = res.astype(BF)
+        keep(mix.at[l], mix_o.at[l])
+        give_rows(ng.at[l, mine, :], l * 4 + 2).start()
+        for j in range(4):
+            gat.until(c0 + 5 + j)
+            load(("u", l, j), wg.at[c0 + 4 + j], wu.at[j])
+            if j == 2:
+                give_rows(ng.at[l, theirs, :], l * 4 + 2).wait_recv()
+            if j >= 2:
+                loads["u", l, j - 2].wait()
+                up(l, j - 2)
+        for j in (2, 3):
+            loads["u", l, j].wait()
+            up(l, j)
+            gat.tick()
+        keep(ng.at[l], ng_o.at[l])
+        keep(hid.at[l], hid_o.at[l])
+        keep(gp.at[l], gp_o.at[l])
+        send.wait_send()
+        for h in range(4):
+            gat.until(c0 + 9 + h)
+            for q in range(2):
+                load(("d", l, h, q), wg.at[c0 + 8 + h, :, :, q * 256:(q + 1) * 256],
+                     wd.at[:, q, :, h * 256:(h + 1) * 256])
+            if h >= 1:
+                for q in range(2):
+                    loads["d", l, h - 1, q].wait()
+                sbuf[:, (h - 1) * 256:h * 256] = down_term(l, theirs, h - 1).astype(BF)
+        for q in range(2):
+            loads["d", l, 3, q].wait()
+        sbuf[:, 768:1024] = down_term(l, theirs, 3).astype(BF)
+        send = remote(sbuf, rbuf.at[l * 2 + 1], x_send.at[l * 4 + 3], x_recv.at[l * 4 + 3], p.peer)
+        send.start()
+        gat.tick()
+        for h in range(4):
+            cols = slice(h * 256, (h + 1) * 256)
+            sec[l, :, cols] = normed[:, cols] + down_term(l, mine, h) + shift(l, 2)[:, cols]
+        gat.tick()
+        gat.tick()
+        send.wait_recv()
+        for i in range(rows // 32):
+            r = slice(i * 32, (i + 1) * 32)
+            second = sec[l, r, :] + rbuf[l * 2 + 1, r, :].astype(F32)
+            sec[l, r, :] = second
+            res = norm_rows(second, gain(l, 1), shift(l, 3))
+            stream[r, :] = res
+            if l + 1 < layers:
+                xg[l + 1, pl.ds(pl.multiple_of(x * rows + i * 32, 32), 32), :] = res.astype(BF)
+        keep(sec.at[l], sec_o.at[l])
+        if l + 1 < layers:
+            give_rows(xg.at[l + 1, mine, :], l * 4 + 4).start()
+    keep(stream, out_o)
+    send.wait_send()
+    gat.finish()
+    for copy in v_far + [v_side, v_twin, v_peer]:
+        copy.wait_send()
+    for l in range(layers):
+        give_rows(xg.at[l, mine, :], l * 4).wait_send()
+        give_rows(ng.at[l, mine, :], l * 4 + 2).wait_send()
+    for copy in outs:
+        copy.wait()
+
+
+def forward_call(depth, layers, rows, wp, vp, tok, segc, segr):
+    group, hw, fh = 2 * rows, 512, 2048
+    vm = pltpu.VMEM
+    saved = [((layers, group, 1024), BF), ((layers, 3, group, hw), BF), ((layers, group, hw), BF),
+             ((layers, 8, group), F32), ((layers, rows, 1024), F32), ((layers, group, 1024), BF),
+             ((layers, group, fh), BF), ((layers, group, fh), BF), ((layers, rows, 1024), F32)]
+    dp = depth * 4
+    n = layers * CH
+    out_shape = [jax.ShapeDtypeStruct((n, dp, 64, 512), BF), jax.ShapeDtypeStruct((32, 2048), F32),
+                 jax.ShapeDtypeStruct((rows, 1024), F32)] + [jax.ShapeDtypeStruct(s, t) for s, t in saved]
+    scratch = [vm((2, depth, 2, 2, 32, 128), F32), vm((32, 2048), F32), vm((rows, 1024), F32), vm((rows, 1024), F32),
+               vm((group, group), F32), vm((2, group, 256), F32), vm((2, group, 256), BF)]
+    scratch += [vm(s, t) for s, t in saved]
+    scratch += [vm((rows, 1024), BF), vm((2 * layers, rows, 1024), BF),
+                vm((3, dp, 64, 512), BF), vm((dp, 32, 1024), BF), vm((4, dp, 64, 512), BF), vm((dp, 2, 64, 1024), BF)]
+    dma = pltpu.SemaphoreType.DMA
+    scratch += [dma((n, depth + 1)), dma((n, depth + 1)), dma((depth + 2,)), dma((depth + 2,)),
+                dma((4 * layers,)), dma((4 * layers,)), dma((17 * layers,)), dma((16 * layers,)), dma]
+    full = pl.BlockSpec(memory_space=pltpu.VMEM)
+    hbm = pl.BlockSpec(memory_space=pl.ANY)
+    return pl.pallas_call(
+        functools.partial(fwd_kernel, depth, layers),
+        out_shape=out_shape,
+        in_specs=[hbm, full, full, full, full],
+        out_specs=[hbm] * len(out_shape),
+        scratch_shapes=scratch,
+        compiler_params=pltpu.CompilerParams(collective_id=1, has_side_effects=True, vmem_limit_bytes=62 * 2**20),
+        cost_estimate=pl.CostEstimate(flops=14 * 10**9, bytes_accessed=60 * 10**6, transcendentals=0),
+    )(wp, vp, tok, segc, segr)
+
+def pack(w_query, w_key, w_value, w_out, w_up, w_down):
+    layers = w_query.shape[0]
+    o = w_out.reshape(layers, 1, 32, 2, 512).transpose(0, 1, 3, 2, 4).reshape(layers, 1, 64, 512)
+    u = w_up.reshape(layers, 64, 4, 512).transpose(0, 2, 1, 3)
+    d = w_down.reshape(layers, 2, 64, 4, 256).transpose(0, 3, 2, 1, 4).reshape(layers, 4, 64, 512)
+    parts = [w_query[:, None], w_key[:, None], w_value[:, None], o, u, d]
+    return jnp.concatenate(parts, axis=1).reshape(layers * CH, 64, 512)
+
+
+def pack_vectors(qv_bias, up_bias, norm_gain, shift_bias):
+    layers = qv_bias.shape[0]
+    dp, x = lax.axis_index("dp"), lax.axis_index("tensor")
+
+    def spread(rows32, slot):
+        tiled = jnp.tile(rows32, (1, 4))
+        lane = lax.broadcasted_iota(jnp.int32, tiled.shape, 1) // 32
+        return jnp.where(lane == slot, tiled, 0.0)
+
+    full = jnp.concatenate([norm_gain.reshape(layers * 2, 32), shift_bias.reshape(layers * 4, 32)])
+    full = spread(full, (dp * 2 + x) % 4)
+    half = spread(qv_bias.astype(F32).reshape(layers * 2, 32), dp % 4)
+    out = jnp.zeros((32, 128), F32)
+    out = out.at[0:layers * 6].set(full)
+    out = out.at[16:16 + layers * 2].set(half)
+    return out.at[24:24 + layers].set(up_bias.astype(F32))
+
+
 def on_device(
+    tokens,
+    cotangent,
+    segment_ids,
+    w_query,
+    w_key,
+    w_value,
+    w_out,
+    w_up,
+    w_down,
+    qv_bias,
+    up_bias,
+    norm_gain,
+    shift_bias,
+):
+    layers = w_query.shape[0]
+    rows = tokens.shape[0]
+    dp = lax.axis_size("dp")
+    wp = pack(w_query, w_key, w_value, w_out, w_up, w_down)
+    vp = pack_vectors(qv_bias, up_bias, norm_gain, shift_bias)
+    (wg, vec, out, xg, qkv, att, lse, mix, ng, hid, gp, sec) = forward_call(
+        dp // 4, layers, rows, wp, vp, tokens, segment_ids[:, None], segment_ids[None, :]
+    )
+    grad = cotangent.astype(F32)
+    mat_shards = [None] * layers
+    vec_shards = [None] * layers
+    segs = segment_ids[None]
+    for l in reversed(range(layers)):
+        c = l * CH
+        w_q, w_k, w_v = (wg[c + i].reshape(1024, 512) for i in range(3))
+        w_o = wg[c + 3].reshape(dp, 2, 32, 512).transpose(0, 2, 1, 3).reshape(512, 1024)
+        w_u = wg[c + 4:c + 8].reshape(4, 1024, 512).transpose(1, 0, 2).reshape(1024, 2048)
+        w_d = wg[c + 8:c + 12].reshape(4, dp, 64, 2, 256).transpose(1, 3, 2, 0, 4).reshape(2048, 1024)
+        mats = (w_q, w_k, w_v, w_o, w_u, w_d, None, None)
+        vecs = (vec[l * 2:l * 2 + 2, :1024], vec[4 + l * 4:8 + l * 4, :1024])
+        kept = (xg[l], qkv[l, 0], qkv[l, 1], qkv[l, 2], att[l], lse[l][None], mix[l], ng[l], gp[l], hid[l], sec[l])
+        grad, mat_grads, vec_grads = backward_layer(grad, mats, vecs, kept, segs, segs.shape[1])
+        dims = (0, 0, 0, 0, 0, 0, 1, 0)
+        mat_shards[l] = tuple(
+            lax.psum_scatter(g.astype(BF), "dp", scatter_dimension=d, tiled=True).astype(F32)
+            for g, d in zip(mat_grads, dims)
+        )
+        vec_shards[l] = tuple(
+            lax.psum_scatter(g, ("dp", "tensor"), scatter_dimension=1, tiled=True) for g in vec_grads
+        )
+
+    def stacked(index, source):
+        return jnp.stack([entry[index] for entry in source])
+
+    return (out, grad) + tuple(stacked(i, mat_shards) for i in range(8)) + tuple(stacked(i, vec_shards) for i in range(2))
+
+
+def on_any_mesh(
     tokens,
     cotangent,
     segment_ids,
@@ -255,7 +821,7 @@
             lax.all_gather(qv_bias[layer], "dp", axis=1, tiled=True),
             lax.all_gather(up_bias[layer], "dp", axis=0, tiled=True),
         )
-        grad, mat_grads, vec_grads = backward_layer(
+        grad, mat_grads, vec_grads = backward_layer_any(
             grad, mats, vecs_all[layer], kept_all[layer], segs, seq
         )
         g_q, g_k, g_v, g_o, g_u, g_d, g_qv, g_ub = mat_grads
@@ -340,6 +906,7 @@
         P(None, None, ("dp", "tensor")),
         P(None, None, ("dp", "tensor")),
     )
+    small = mesh.shape["tensor"] == 2 and mesh.shape["dp"] == 16
     return jax.shard_map(
-        on_device, mesh=mesh, in_specs=in_specs, out_specs=out_specs, check_vma=False
-    )
+        on_device if small else on_any_mesh, mesh=mesh, in_specs=in_specs, out_specs=out_specs, check_vma=False
+    )

time: 2660 us -> 1960 us (0.74)
  waiting for transfers between devices: 1890 us -> 1390 us
  blocking collectives: 385 us -> 30 us
  Pallas kernels: 0 us -> 246 us
  matrix products: 183 us -> 115 us
    all_gather x16 -> x0, waiting for transfers between devices: 396 us -> none  [the longest x2 75.7 us: on_device(): lax.all_gather(w_query[layer], 'dp', axis=0, tiled=True)]
    unnamed x58 -> x32, waiting for transfers between devices: 889 us -> 529 us
    all_gather x8 -> x0, blocking collectives: 355 us -> none  [the longest x2 141 us: on_device(): lax.all_gather(norm_gain[layer], ('dp', 'tensor'), axis=1, tiled=True)]
    reduce_scatter x10 -> x12, waiting for transfers between devices: 454 us -> 774 us  [on_device(): lax.psum_scatter(g.astype(BF), 'dp', scatter_dimension=d, tiled=True)]
    pallas_call x0 -> x1, Pallas kernels: none -> 246 us  [forward_call(): pl.pallas_call(functools.partial(fwd_kernel, depth, layers), out_shape=ou...]
    dot_general x16 -> x2, matrix products: 75.1 us -> 10.3 us  [attend_back(): jnp.einsum('qhd,khd->hqk', query, key, preferred_element_type=jnp.float32)]
    all_gather x4, waiting for transfers between devices: 72.4 us -> 10.7 us  [gather_grads(): return lax.all_gather(rows, 'tensor', axis=0, tiled=True)]
    reshape x0 -> x9, local copies, waits for them, and re-layouts: none -> 41.2 us  [the longest x4 25.8 us: on_device(): wg[c + 8:c + 12].reshape(4, dp, 64, 2, 256).transpose(1, 3, 2, 0, 4)]
  transfers between devices with their start and end apart: 46 -> 26, of which waited for: 42 -> 24; matrix products, arithmetic and copies ran while one was open for 9% -> 10% of each run, Pallas kernels for 0% -> 0%
where the time goes in v1:
time: 1960 us; the launch traced here: 1950 us
  waiting for transfers between devices  1390 us (71%)
  Pallas kernels  246 us (13%)
  matrix products  115 us (6%)
  local copies, waits for them, and re-layouts  114 us (6%)
  other arithmetic  41 us (2%)
  blocking collectives  30 us (2%)
    reduce_scatter x12, waiting for transfers between devices, on_device(): lax.psum_scatter(g.astype(BF), 'dp', scatter_dimension=d, tiled=True)  774 us
    unnamed x32, waiting for transfers between devices  529 us
    pallas_call x1, Pallas kernels, forward_call(): pl.pallas_call(functools.partial(fwd_kernel, depth, layers), out_shape=ou...  246 us
    reduce_scatter x4, waiting for transfers between devices, sum_grads(): lax.psum_scatter(term(jnp.int32(0), lax.axis_size('tensor') * rows).astyp...  74.8 us
    dot_general x12, matrix products, inner(): lax.dot_general(left, right, (((0,), (0,)), ((), ())), preferred_element_...  46.8 us
  transfers between devices with their start and end apart: 26, of which 24 were waited for; matrix products, arithmetic and copies ran while one was open for 10% of the time, Pallas kernels for 0%

profile of v1, /device:TPU:0, one launch (start us, length us, event | category | flops | bytes accessed | tf_op | source)
XLA Modules:
  0.0 1952.1 jit_solution(14372252364755872444)
XLA Ops:
  19.2 245.7 %shard_map.220 = (bf16[24,16,64,512]{3,2,1,0:T(8,128)(2,1)}, f32[32,2048]{1,0:T(8,128)}, f32[256,1024]{1,0:T(8,128)}, bf16[2,512,1024]{2,1,0:T(8,128)(2,1)}, bf1...) custom-call(bf16[24,64,512]{2,1,0:T(8,128)(2,1)} %bitcast.386, ...), custom_call_target="tpu_custom_call" | custom-call | flops 14000000000 | bytes 60000000 | tf_op jit(solution)/shard_map/pallas_call | solution.py:679
  271.4 12.8 fusion.66
  284.2 6.9 reshape.385
  291.2 5.7 copy.79
  300.0 6.3 copy.80
  306.3 5.7 fusion.69
  313.3 3.3 convolution_convert_fusion.13
  317.2 6.0 fusion.65
  323.3 13.3 reduce-scatter.35.cloned.1.call-done
  341.5 3.6 fusion.67
  353.8 5.7 fusion.71
  365.2 5.8 bitcast_reduce_fusion.2
  382.4 20.4 %reduce-scatter.37.cloned.1.call-done = bf16[256,1024]{1,0:T(8,128)(2,1)} async-done(((bf16[512,1024]{1,0:T(8,128)(2,1)}), bf16[256,1024]{1,0:T(8,128)(2,1)}) %reduce-scatter.37.cloned.1.call-update) | async-done | bytes 524304 | tf_op jit(solution)/shard_map/reduce_scatter | solution.py:60
  408.7 7.2 reshape.393
  415.9 5.9 copy.88
  424.8 6.3 copy.89
  431.1 5.7 fusion.70
  438.2 3.3 convolution_convert_fusion.12
  441.6 20.4 %reduce-scatter.39.cloned.1.call-done = bf16[256,1024]{1,0:T(8,128)(2,1)} async-done(((bf16[512,1024]{1,0:T(8,128)(2,1)}), bf16[256,1024]{1,0:T(8,128)(2,1)}) %reduce-scatter.39.cloned.1.call-update) | async-done | bytes 524304 | tf_op jit(solution)/shard_map/reduce_scatter | solution.py:60
  470.9 4.6 fusion.74
  481.1 7.5 all-gather.11.cloned.1.call-done
  490.6 5.6 bitcast_reduce_fusion
  496.3 5.2 multiply_reduce_fusion
  524.6 3.7 fusion.23
  542.1 5.9 convolution_convert_fusion
  549.2 5.9 convolution_convert_fusion.1
  556.8 6.0 convolution_convert_fusion.2
  562.8 5.9 convolution_convert_fusion.3
  570.6 54.3 %reduce-scatter.73.cloned.1.call-done = f32[32,2]{1,0:T(8,128)} async-done(((f32[1024,2]{1,0:T(8,128)}), f32[32,2]{1,0:T(8,128)}) %reduce-scatter.73.cloned.1.call-update) | async-done | bytes 272
  625.7 54.3 %reduce-scatter.69.cloned.1.call-done = bf16[32,2]{1,0:T(8,128)(2,1)} async-done(((bf16[512,2]{1,0:T(8,128)(2,1)}), bf16[32,2]{1,0:T(8,128)(2,1)}) %reduce-scatter.69.cloned.1.call-update) | async-done | bytes 144
  680.8 134.4 %reduce-scatter.77.cloned.1.call-done = f32[32,4]{1,0:T(8,128)} async-done(((f32[1024,4]{1,0:T(8,128)}), f32[32,4]{1,0:T(8,128)}) %reduce-scatter.77.cloned.1.call-update) | async-done | bytes 528
  816.0 30.0 %all-reduce.3 = (bf16[2048]{0:T(1024)(128)(2,1)S(1)}, bf16[2048]{0:T(1024)(128)(2,1)S(1)}) all-reduce(bf16[2048]{0:T(1024)(128)(2,1)S(1)} %get-tuple-element.201, bf16[2048]{0:T(1024)(128)(2,1)S(1)} %get-tuple-element.203), channel_id=21, replica_groups=mesh['dp'=16,'tensor'=2] {'dp'}, use_global_device_ids=true, to_apply=%region_43.44.clone | all-reduce | flops 4096 | bytes 16384
  846.8 100.8 %reduce-scatter.71.cloned.1.call-done = f32[32,2]{1,0:T(8,128)} async-done(((f32[1024,2]{1,0:T(8,128)}), f32[32,2]{1,0:T(8,128)}) %reduce-scatter.71.cloned.1.call-update) | async-done | bytes 272
  949.0 130.7 %reduce-scatter.75.cloned.1.call-done = f32[32,4]{1,0:T(8,128)} async-done(((f32[1024,4]{1,0:T(8,128)}), f32[32,4]{1,0:T(8,128)}) %reduce-scatter.75.cloned.1.call-update) | async-done | bytes 528
  1081.1 54.0 %reduce-scatter.67.cloned.1.call-done = bf16[32,2]{1,0:T(8,128)(2,1)} async-done(((bf16[512,2]{1,0:T(8,128)(2,1)}), bf16[32,2]{1,0:T(8,128)(2,1)}) %reduce-scatter.67.cloned.1.call-update) | async-done | bytes 144
  1136.5 59.0 %reduce-scatter.57.cloned.1.call-done = bf16[32,1024]{1,0:T(8,128)(2,1)} async-done(((bf16[512,1024]{1,0:T(8,128)(2,1)}), bf16[32,1024]{1,0:T(8,128)(2,1)}) %reduce-scatter.57.cloned.1.call-update) | async-done | bytes 65552 | tf_op jit(solution)/shard_map/reduce_scatter | solution.py:755
  1195.5 59.9 %reduce-scatter.55.cloned.1.call-done = bf16[32,1024]{1,0:T(8,128)(2,1)} async-done(((bf16[512,1024]{1,0:T(8,128)(2,1)}), bf16[32,1024]{1,0:T(8,128)(2,1)}) %reduce-scatter.55.cloned.1.call-update) | async-done | bytes 65552 | tf_op jit(solution)/shard_map/reduce_scatter | solution.py:755
  1257.0 58.7 %reduce-scatter.53.cloned.1.call-done = bf16[64,512]{1,0:T(8,128)(2,1)} async-done(((bf16[1024,512]{1,0:T(8,128)(2,1)}), bf16[64,512]{1,0:T(8,128)(2,1)}) %reduce-scatter.53.cloned.1.call-update) | async-done | bytes 65552 | tf_op jit(solution)/shard_map/reduce_scatter | solution.py:755
  1315.7 59.9 %reduce-scatter.51.cloned.1.call-done = bf16[64,512]{1,0:T(8,128)(2,1)} async-done(((bf16[1024,512]{1,0:T(8,128)(2,1)}), bf16[64,512]{1,0:T(8,128)(2,1)}) %reduce-scatter.51.cloned.1.call-update) | async-done | bytes 65552 | tf_op jit(solution)/shard_map/reduce_scatter | solution.py:755
  1377.2 58.7 %reduce-scatter.49.cloned.1.call-done = bf16[64,512]{1,0:T(8,128)(2,1)} async-done(((bf16[1024,512]{1,0:T(8,128)(2,1)}), bf16[64,512]{1,0:T(8,128)(2,1)}) %reduce-scatter.49.cloned.1.call-update) | async-done | bytes 65552 | tf_op jit(solution)/shard_map/reduce_scatter | solution.py:755
  1435.9 60.1 %reduce-scatter.47.cloned.1.call-done = bf16[64,512]{1,0:T(8,128)(2,1)} async-done(((bf16[1024,512]{1,0:T(8,128)(2,1)}), bf16[64,512]{1,0:T(8,128)(2,1)}) %reduce-scatter.47.cloned.1.call-update) | async-done | bytes 65552 | tf_op jit(solution)/shard_map/reduce_scatter | solution.py:755
  1497.7 58.7 %reduce-scatter.45.cloned.1.call-done = bf16[64,512]{1,0:T(8,128)(2,1)} async-done(((bf16[1024,512]{1,0:T(8,128)(2,1)}), bf16[64,512]{1,0:T(8,128)(2,1)}) %reduce-scatter.45.cloned.1.call-update) | async-done | bytes 65552 | tf_op jit(solution)/shard_map/reduce_scatter | solution.py:755
  1556.4 60.1 %reduce-scatter.43.cloned.1.call-done = bf16[64,512]{1,0:T(8,128)(2,1)} async-done(((bf16[1024,512]{1,0:T(8,128)(2,1)}), bf16[64,512]{1,0:T(8,128)(2,1)}) %reduce-scatter.43.cloned.1.call-update) | async-done | bytes 65552 | tf_op jit(solution)/shard_map/reduce_scatter | solution.py:755
  1618.0 20.7 %reduce-scatter.41.cloned.1.call-done = bf16[256,1024]{1,0:T(8,128)(2,1)} async-done(((bf16[512,1024]{1,0:T(8,128)(2,1)}), bf16[256,1024]{1,0:T(8,128)(2,1)}) %reduce-scatter.41.cloned.1.call-update) | async-done | bytes 524304 | tf_op jit(solution)/shard_map/reduce_scatter | solution.py:60
  1640.9 74.4 %reduce-scatter.65.cloned.1.call-done = bf16[128,1024]{1,0:T(8,128)(2,1)} async-done(((bf16[2048,1024]{1,0:T(8,128)(2,1)}), bf16[128,1024]{1,0:T(8,128)(2,1)}) %reduce-scatter.65.cloned.1.call-update) | async-done | bytes 262160 | tf_op jit(solution)/shard_map/reduce_scatter | solution.py:755
  1715.3 75.6 %reduce-scatter.63.cloned.1.call-done = bf16[128,1024]{1,0:T(8,128)(2,1)} async-done(((bf16[2048,1024]{1,0:T(8,128)(2,1)}), bf16[128,1024]{1,0:T(8,128)(2,1)}) %reduce-scatter.63.cloned.1.call-update) | async-done | bytes 262160 | tf_op jit(solution)/shard_map/reduce_scatter | solution.py:755
  1793.0 73.6 %reduce-scatter.61.cloned.1.call-done = bf16[64,2048]{1,0:T(8,128)(2,1)} async-done(((bf16[1024,2048]{1,0:T(8,128)(2,1)}), bf16[64,2048]{1,0:T(8,128)(2,1)}) %reduce-scatter.61.cloned.1.call-update) | async-done | bytes 262160 | tf_op jit(solution)/shard_map/reduce_scatter | solution.py:755
  1866.5 75.8 %reduce-scatter.59.cloned.1.call-done = bf16[64,2048]{1,0:T(8,128)(2,1)} async-done(((bf16[1024,2048]{1,0:T(8,128)(2,1)}), bf16[64,2048]{1,0:T(8,128)(2,1)}) %reduce-scatter.59.cloned.1.call-update) | async-done | bytes 262160 | tf_op jit(solution)/shard_map/reduce_scatter | solution.py:755
  (292 shorter events, 141.8 us)
Async XLA Ops:
  7.2 8.3 copy-start.43
  7.2 8.3 copy-start.36
  7.2 9.0 copy-start.37
  7.2 10.3 copy-start.31
  7.2 299.1 %all-gather.5.cloned.1.call-start = ((), (), s32[]{:S(2)}) async-start(), calls=%async_computation.22 | async-start | bytes 1572864 | tf_op jit(solution)/shard_map/all_gather | solution.py:47
  19.2 250.0 %copy-start.19 = (bf16[256,1024]{1,0:T(8,128)(2,1)S(1)}, bf16[256,1024]{1,0:T(8,128)(2,1)}, u32[]{:S(2)}) copy-start(bf16[256,1024]{1,0:T(8,128)(2,1)} %param.20) | copy-start | bytes 1572868
  270.3 66.3 %copy-start.5 = (f32[256,1024]{1,0:T(8,128)}, f32[256,1024]{1,0:T(8,128)S(1)}, u32[]{:S(2)}) copy-start(f32[256,1024]{1,0:T(8,128)S(1)} %get-tuple-element.162) | copy-start | bytes 3145732
  271.4 65.2 %reduce-scatter.35.cloned.1.call-start = ((), (), s32[]{:S(2)}) async-start(), calls=%async_computation.23 | async-start | bytes 1572864 | tf_op jit(solution)/shard_map/reduce_scatter | solution.py:60
  306.3 7.1 copy-start.16
  316.7 46.0 %all-gather.7.cloned.1.call-start = ((), (), s32[]{:S(2)}) async-start(), calls=%async_computation.24 | async-start | bytes 1572864 | tf_op jit(solution)/shard_map/all_gather | solution.py:47
  341.2 61.6 %reduce-scatter.37.cloned.1.call-start = ((), (), s32[]{:S(2)}) async-start(), calls=%async_computation.25 | async-start | bytes 1572864 | tf_op jit(solution)/shard_map/reduce_scatter | solution.py:60
  345.1 8.5 copy-start.38
  345.1 8.5 copy-start.39
  362.7 8.3 slice-start.2
  365.1 5.8 slice-start.3
  371.0 9.6 copy-start.32
  382.4 48.8 %all-gather.9.cloned.1.call-start = ((), (), s32[]{:S(2)}) async-start(), calls=%async_computation.26 | async-start | bytes 1572864 | tf_op jit(solution)/shard_map/all_gather | solution.py:47
  408.6 53.3 %reduce-scatter.39.cloned.1.call-start = ((), (), s32[]{:S(2)}) async-start(), calls=%async_computation.27 | async-start | bytes 1572864 | tf_op jit(solution)/shard_map/reduce_scatter | solution.py:60
  431.1 7.1 copy-start.15
  438.2 23.8 %copy-start.4 = (f32[256,1024]{1,0:T(8,128)S(1)}, f32[256,1024]{1,0:T(8,128)}, u32[]{:S(2)}) copy-start(f32[256,1024]{1,0:T(8,128)} %copy-done.3) | copy-start | bytes 3145732
  441.5 47.1 %all-gather.11.cloned.1.call-start = ((), (), s32[]{:S(2)}) async-start(), calls=%async_computation.28 | async-start | bytes 1572864 | tf_op jit(solution)/shard_map/all_gather | solution.py:47
  467.2 157.7 %reduce-scatter.73.cloned.1.call-start = ((), (), s32[]{:S(2)}) async-start(), calls=%async_computation.45 | async-start | bytes 540672
  476.6 203.4 %reduce-scatter.69.cloned.1.call-start = ((), (), s32[]{:S(2)}) async-start(), calls=%async_computation.43 | async-start | bytes 139264
  477.6 337.6 %reduce-scatter.77.cloned.1.call-start = ((), (), s32[]{:S(2)}) async-start(), calls=%async_computation.47 | async-start | bytes 540672
  478.8 468.8 %reduce-scatter.71.cloned.1.call-start = ((), (), s32[]{:S(2)}) async-start(), calls=%async_computation.44 | async-start | bytes 540672
  479.9 599.8 %reduce-scatter.75.cloned.1.call-start = ((), (), s32[]{:S(2)}) async-start(), calls=%async_computation.46 | async-start | bytes 540672
  481.1 654.1 %reduce-scatter.67.cloned.1.call-start = ((), (), s32[]{:S(2)}) async-start(), calls=%async_computation.42 | async-start | bytes 139264
  496.2 22.3 %copy-start.34 = (bf16[8,64,512]{2,1,0:T(8,128)(2,1)}, bf16[8,64,512]{2,1,0:T(8,128)(2,1)S(1)}, u32[]{:S(2)}) copy-start(bf16[8,64,512]{2,1,0:T(8,128)(2,1)S(1)} %get-tuple-element.198) | copy-start | bytes 1572868
  496.3 6.0 slice-start.1
  507.8 25.6 %copy-start.24 = (bf16[8,64,512]{2,1,0:T(8,128)(2,1)}, bf16[8,64,512]{2,1,0:T(8,128)(2,1)S(1)}, u32[]{:S(2)}) copy-start(bf16[8,64,512]{2,1,0:T(8,128)(2,1)S(1)} %get-tuple-element.200) | copy-start | bytes 1572868
  508.7 6.6 copy-start.33
  508.8 686.7 %reduce-scatter.57.cloned.1.call-start = ((), (), s32[]{:S(2)}) async-start(), calls=%async_computation.37 | async-start | bytes 1114112 | tf_op jit(solution)/shard_map/reduce_scatter | solution.py:755
  512.0 743.4 %reduce-scatter.55.cloned.1.call-start = ((), (), s32[]{:S(2)}) async-start(), calls=%async_computation.36 | async-start | bytes 1114112 | tf_op jit(solution)/shard_map/reduce_scatter | solution.py:755
  515.1 800.6 %reduce-scatter.53.cloned.1.call-start = ((), (), s32[]{:S(2)}) async-start(), calls=%async_computation.35 | async-start | bytes 1114112 | tf_op jit(solution)/shard_map/reduce_scatter | solution.py:755
  515.4 6.2 copy-start.23
  518.4 857.2 %reduce-scatter.51.cloned.1.call-start = ((), (), s32[]{:S(2)}) async-start(), calls=%async_computation.34 | async-start | bytes 1114112 | tf_op jit(solution)/shard_map/reduce_scatter | solution.py:755
  521.5 914.4 %reduce-scatter.49.cloned.1.call-start = ((), (), s32[]{:S(2)}) async-start(), calls=%async_computation.33 | async-start | bytes 1114112 | tf_op jit(solution)/shard_map/reduce_scatter | solution.py:755
  524.6 971.5 %reduce-scatter.47.cloned.1.call-start = ((), (), s32[]{:S(2)}) async-start(), calls=%async_computation.32 | async-start | bytes 1114112 | tf_op jit(solution)/shard_map/reduce_scatter | solution.py:755
  530.2 6.4 copy-start.11
  530.2 1026.2 %reduce-scatter.45.cloned.1.call-start = ((), (), s32[]{:S(2)}) async-start(), calls=%async_computation.31 | async-start | bytes 1114112 | tf_op jit(solution)/shard_map/reduce_scatter | solution.py:755
  533.3 1083.1 %reduce-scatter.43.cloned.1.call-start = ((), (), s32[]{:S(2)}) async-start(), calls=%async_computation.30 | async-start | bytes 1114112 | tf_op jit(solution)/shard_map/reduce_scatter | solution.py:755
  536.5 1102.2 %reduce-scatter.41.cloned.1.call-start = ((), (), s32[]{:S(2)}) async-start(), calls=%async_computation.29 | async-start | bytes 1572864 | tf_op jit(solution)/shard_map/reduce_scatter | solution.py:60
  542.1 1173.3 %reduce-scatter.65.cloned.1.call-start = ((), (), s32[]{:S(2)}) async-start(), calls=%async_computation.41 | async-start | bytes 4456448 | tf_op jit(solution)/shard_map/reduce_scatter | solution.py:755
  548.0 1242.8 %reduce-scatter.63.cloned.1.call-start = ((), (), s32[]{:S(2)}) async-start(), calls=%async_computation.40 | async-start | bytes 4456448 | tf_op jit(solution)/shard_map/reduce_scatter | solution.py:755
  555.2 1311.3 %reduce-scatter.61.cloned.1.call-start = ((), (), s32[]{:S(2)}) async-start(), calls=%async_computation.39 | async-start | bytes 4456448 | tf_op jit(solution)/shard_map/reduce_scatter | solution.py:755
  562.7 1379.5 %reduce-scatter.59.cloned.1.call-start = ((), (), s32[]{:S(2)}) async-start(), calls=%async_computation.38 | async-start | bytes 4456448 | tf_op jit(solution)/shard_map/reduce_scatter | solution.py:755
  568.7 1070.0 %copy-start.7 = (f32[256,1024]{1,0:T(8,128)S(1)}, f32[256,1024]{1,0:T(8,128)}, u32[]{:S(2)}) copy-start(f32[256,1024]{1,0:T(8,128)} %copy-done.6) | copy-start | bytes 3145732
  568.8 1375.6 %copy-start.30 = (f32[256,1024]{1,0:T(8,128)S(1)}, f32[256,1024]{1,0:T(8,128)}, u32[]{:S(2)}) copy-start(f32[256,1024]{1,0:T(8,128)} %get-tuple-element.219) | copy-start | bytes 3145732
  (31 other events, 89.3 us)
Sparse Core Ops, SparseCore 0:
  271.5 20.6 all-gather.4
  316.8 19.6 reduce-scatter.34
  341.3 21.3 all-gather.6
  382.5 20.3 reduce-scatter.36
  408.8 21.2 all-gather.8
  441.6 20.2 reduce-scatter.38
  467.3 21.3 all-gather.10
  491.0 133.8 reduce-scatter.72
  628.9 51.0 reduce-scatter.68
  682.1 133.0 reduce-scatter.76
  817.6 129.9 reduce-scatter.70
  949.7 129.9 reduce-scatter.74
  1084.1 50.9 reduce-scatter.66
  1139.0 56.3 reduce-scatter.56
  1198.9 56.4 reduce-scatter.54
  1259.3 56.3 reduce-scatter.52
  1319.2 56.4 reduce-scatter.50
  1379.6 56.3 reduce-scatter.48
  1439.5 56.4 reduce-scatter.46
  1500.0 56.3 reduce-scatter.44
  1560.0 56.3 reduce-scatter.42
  1619.3 19.3 reduce-scatter.40
  1642.6 72.7 reduce-scatter.64
  1719.5 71.3 reduce-scatter.62
  1794.7 71.7 reduce-scatter.60
  1870.7 71.5 reduce-scatter.58
